TPU v7x, 256 devices: a whole 4x4x8 slice. The times are simulated.
256 devices in a mesh: group: 8 (over z), dev: 32 (over y, x, core).
Axes of the slice: x: 4, y: 4, z: 8, core: 2. Of those that a mesh axis runs over, the one named last changes fastest.
Arguments:
- fine_state: float32 [5, 256, 65536], P(None, 'group', 'dev'), may hold values from -2 to 9.25, as said below
- coarse_boxes: float32 [32768, 5, 512], P(('group', 'dev')), may hold values from -2 to 9.25, as said below
- piece_owner: int32 [8192, 1], P(('group', 'dev')), may hold values from 0 to 31; in each aligned block of 32 rows (0 to 31, 32 to 63, ...) at most 4 rows name the same one
- piece_box: int32 [8192], P(('group', 'dev')), may hold values from 0 to 127
Outputs:
- fine_next: float32 [5, 256, 65536], P(None, 'group', 'dev')
- flux_register: float32 [5, 32, 32768], P(None, None, ('group', 'dev'))
Inputs may be any that keep to these rules, and one draw needn't show every extreme that they name: `piece_owner`: among the pieces of one device no owner is named more than 4 times, and in some devices one owner is named exactly 4 times. `fine_state`: conserved variables of states with density in 0.5 to 2, velocity components in -1 to 1 and pressure in 0.4 to 2.5. `coarse_boxes`: conserved variables of states with density in 0.5 to 2, velocity components in -1 to 1 and pressure in 0.4 to 2.5.
All inputs are finite; a program needn't handle non-finite values.
Results may differ from a plain program's by a relative error of at most 0.0003.
Values sent between devices are 32-bit elements; how exact they have to be, the bound alone decides.
A program may use at most 128 MiB of HBM per device.

v0:
```python
import jax
import jax.numpy as jnp
from jax import lax
from jax.sharding import PartitionSpec as P

PS = 16
RATIO = 4
QS = 16
PATCH_Y = 2
PATCH_X = 8
BOX_DEV = 128
CF = 4
CB = 8


GAMMA = 1.4
DT_DX = 0.08


def with_halo(block, sides, width, periodic):
    for axis, dim in sides:
        count = lax.axis_size(axis)
        forward = [(i, i + 1) for i in range(count - 1)]
        if periodic:
            forward.append((count - 1, 0))
        backward = [(target, source) for source, target in forward]
        low = lax.ppermute(
            lax.slice_in_dim(block, block.shape[dim] - width, None, axis=dim), axis, forward
        )
        high = lax.ppermute(lax.slice_in_dim(block, 0, width, axis=dim), axis, backward)
        block = jnp.concatenate([low, block, high], axis=dim)
    return block


def minmod(lower_diff, upper_diff):
    return jnp.where(
        lower_diff * upper_diff > 0.0,
        jnp.where(jnp.abs(lower_diff) < jnp.abs(upper_diff), lower_diff, upper_diff),
        0.0,
    )


def to_primitive(conserved):
    density = conserved[0]
    momentum = conserved[1:4]
    kinetic = (
        0.5
        * (momentum[0] * momentum[0] + momentum[1] * momentum[1] + momentum[2] * momentum[2])
        / density
    )
    pressure = (GAMMA - 1.0) * (conserved[4] - kinetic)
    return jnp.stack(
        [density, momentum[0] / density, momentum[1] / density, momentum[2] / density, pressure]
    )


def state_terms(primitive, normal):
    density = primitive[0]
    pressure = primitive[4]
    normal_speed = primitive[1 + normal]
    energy = pressure / (GAMMA - 1.0) + 0.5 * density * (
        primitive[1] * primitive[1] + primitive[2] * primitive[2] + primitive[3] * primitive[3]
    )
    cons_list = [
        density,
        density * primitive[1],
        density * primitive[2],
        density * primitive[3],
        energy,
    ]
    flux_list = [element * normal_speed for element in cons_list]
    flux_list[1 + normal] = flux_list[1 + normal] + pressure
    flux_list[4] = flux_list[4] + pressure * normal_speed
    sound_speed = jnp.sqrt(GAMMA * pressure / density)
    return (jnp.stack(cons_list), jnp.stack(flux_list), normal_speed, sound_speed)


def hll_flux(lower_state, upper_state, normal):
    cons_low, flux_low, speed_low, sound_low = state_terms(lower_state, normal)
    cons_up, flux_up, speed_up, sound_up = state_terms(upper_state, normal)
    slowest = jnp.minimum(jnp.minimum(speed_low - sound_low, speed_up - sound_up), 0.0)
    fastest = jnp.maximum(jnp.maximum(speed_low + sound_low, speed_up + sound_up), 0.0)
    return (fastest * flux_low - slowest * flux_up + slowest * fastest * (cons_up - cons_low)) / (
        fastest - slowest
    )


def face_fluxes(primitive, lower_ghost, upper_ghost, dim_index, normal):
    length = primitive.shape[dim_index]

    def part_of(array, start, stop):
        return lax.slice_in_dim(array, start, stop, axis=dim_index)

    before = jnp.concatenate(
        [part_of(lower_ghost, 1, 2), part_of(primitive, 0, length - 1)], axis=dim_index
    )
    before_two = jnp.concatenate([lower_ghost, part_of(primitive, 0, length - 2)], axis=dim_index)
    after = jnp.concatenate(
        [part_of(primitive, 1, length), part_of(upper_ghost, 0, 1)], axis=dim_index
    )
    slopes = minmod(primitive - before, after - primitive)
    slopes_before = minmod(before - before_two, primitive - before)
    lower_faces = hll_flux(before + 0.5 * slopes_before, primitive - 0.5 * slopes, normal)
    last_cell = part_of(primitive, length - 1, length)
    ghost_near = part_of(upper_ghost, 0, 1)
    ghost_far = part_of(upper_ghost, 1, 2)
    ghost_slope = minmod(ghost_near - last_cell, ghost_far - ghost_near)
    end_face = hll_flux(
        last_cell + 0.5 * part_of(slopes, length - 1, length),
        ghost_near - 0.5 * ghost_slope,
        normal,
    )
    upper_faces = jnp.concatenate([part_of(lower_faces, 1, length), end_face], axis=dim_index)
    return (upper_faces - lower_faces, lower_faces, end_face)


def advance(primitive, x_low, x_high, y_low, y_high, z_low, z_high):
    change = (
        face_fluxes(primitive, x_low, x_high, 3, 0)[0]
        + face_fluxes(primitive, y_low, y_high, 1, 1)[0]
    )
    z_change, z_lower, z_end = face_fluxes(primitive, z_low, z_high, 2, 2)
    return (change + z_change, z_lower[:, :, 0, :], z_end[:, :, 0, :])


def extract(box_cells, face_side):
    shaped = box_cells.reshape(box_cells.shape[:-1] + (CB, CB, CB))
    low_cut = shaped[..., CB - 4 : CB - 1, 1 : CB - 1, 1 : CB - 1]
    high_cut = shaped[..., 1:4, 1 : CB - 1, 1 : CB - 1]
    return jnp.where((face_side == 1)[..., None, None, None, None], high_cut, low_cut)


def spread(values):
    return values[..., None, :, None, :, None]


def interpolate(coarse_cut, face_side):
    moved = jnp.moveaxis(coarse_cut, -4, 0)
    primitive = to_primitive(moved)
    centre = primitive[..., 1, 1:-1, 1:-1]
    slope_z = minmod(centre - primitive[..., 0, 1:-1, 1:-1], primitive[..., 2, 1:-1, 1:-1] - centre)
    slope_y = minmod(centre - primitive[..., 1, :-2, 1:-1], primitive[..., 1, 2:, 1:-1] - centre)
    slope_x = minmod(centre - primitive[..., 1, 1:-1, :-2], primitive[..., 1, 1:-1, 2:] - centre)
    offsets = (jnp.arange(RATIO, dtype=jnp.float32) + 0.5) / RATIO - 0.5
    z_offsets = jnp.where((face_side == 1)[..., None], offsets[:2], offsets[RATIO - 2 :])
    fine = spread(centre) + spread(slope_z) * z_offsets[..., :, None, None, None, None]
    fine = fine + spread(slope_y) * offsets[:, None, None]
    fine = fine + spread(slope_x) * offsets
    fine = fine.reshape(fine.shape[:-5] + (2, QS, QS))
    return jnp.moveaxis(fine, 0, -4)


def assemble(pieces, face_index):
    chosen = pieces[:, :, face_index]
    return chosen.transpose(4, 0, 3, 6, 5, 1, 2, 7).reshape(5, PATCH_Y * PS, 2, PATCH_X * PS)


def coarsen(flux):
    across = PS // QS
    grouped = flux.reshape(5, PATCH_Y, across, CF, RATIO, PATCH_X, across, CF, RATIO)
    summed = grouped.sum(axis=(4, 8)) * (1.0 / RATIO)
    return summed.transpose(1, 4, 5, 2, 0, 3, 6)


def local(fine_state, coarse_boxes, piece_owner, piece_box):
    members = lax.axis_size("dev")
    dev_index = lax.axis_index("dev")
    y_cells = fine_state.shape[1]
    x_cells = fine_state.shape[2] // PS
    across = PS // QS
    conserved = fine_state.reshape(5, y_cells, x_cells, PS).transpose(0, 1, 3, 2)
    primitive = to_primitive(conserved)
    x_edges = jnp.concatenate([primitive[..., :2], primitive[..., x_cells - 2 :]], axis=3)
    x_wide = with_halo(x_edges, (("dev", 3),), 2, False)
    first_cell = primitive[..., :1]
    last_cell = primitive[..., x_cells - 1 :]
    x_low = jnp.where(
        dev_index == 0, jnp.concatenate([first_cell, first_cell], axis=3), x_wide[..., :2]
    )
    x_high = jnp.where(
        dev_index == members - 1, jnp.concatenate([last_cell, last_cell], axis=3), x_wide[..., 6:]
    )
    y_edges = jnp.concatenate([primitive[:, :2], primitive[:, y_cells - 2 :]], axis=1)
    y_wide = with_halo(y_edges, (("group", 1),), 2, True)
    y_low = y_wide[:, :2]
    y_high = y_wide[:, 6:]
    piece_count = piece_box.shape[0]
    capacity = max(4, 2 * piece_count // members)
    owners = piece_owner[:, 0]
    local_ids = jnp.arange(piece_count, dtype=jnp.int32)
    face_side = local_ids // (across * across) % 2
    request_value = piece_box + BOX_DEV * face_side
    owner_hot = (owners[:, None] == jnp.arange(members, dtype=jnp.int32)[None, :]).astype(jnp.int32)
    earlier = jnp.cumsum(owner_hot, axis=0) - owner_hot
    ranks = jnp.sum(earlier * owner_hot, axis=1)
    slot_ids = owners * capacity + ranks
    slot_hot = slot_ids[:, None] == jnp.arange(members * capacity, dtype=jnp.int32)[None, :]
    requests = (jnp.sum(jnp.where(slot_hot, request_value[:, None] + 1, 0), axis=0) - 1).reshape(
        members, capacity
    )
    received = lax.all_to_all(requests, "dev", split_axis=0, concat_axis=0, tiled=True)
    slot_live = received >= 0
    box_local = jnp.where(slot_live, received % BOX_DEV, 0)
    served_side = jnp.where(slot_live, received // BOX_DEV, 0)
    coarse_cut = extract(coarse_boxes[box_local], served_side)
    payload = jnp.where(
        slot_live[..., None, None, None, None], interpolate(coarse_cut, served_side), 0.0
    )
    back = lax.all_to_all(payload, "dev", split_axis=0, concat_axis=0, tiled=True)
    flat = back.reshape((members * capacity,) + back.shape[2:])
    mine = flat[slot_ids]
    pieces = mine.reshape(PATCH_Y, PATCH_X, 2, across, across, 5, 2, QS, QS)
    z_low = assemble(pieces, 0)
    z_high = assemble(pieces, 1)
    change, bottom_flux, top_flux = advance(primitive, x_low, x_high, y_low, y_high, z_low, z_high)
    fine_next = (conserved - DT_DX * change).transpose(0, 1, 3, 2).reshape(5, y_cells, x_cells * PS)
    register_terms = jnp.stack([coarsen(bottom_flux), coarsen(top_flux)], axis=2).reshape(
        piece_count, 5 * CF * CF
    )
    outgoing = jnp.dot(
        slot_hot.astype(jnp.float32).T,
        register_terms,
        precision=lax.Precision.HIGHEST,
        preferred_element_type=jnp.float32,
    )
    incoming = lax.all_to_all(
        outgoing.reshape(members, capacity, 5 * CF * CF),
        "dev",
        split_axis=0,
        concat_axis=0,
        tiled=True,
    )
    targets = received.reshape(members * capacity)
    target_hot = (targets[:, None] == jnp.arange(2 * BOX_DEV, dtype=jnp.int32)[None, :]).astype(
        jnp.float32
    )
    summed = jnp.dot(
        incoming.reshape(members * capacity, 5 * CF * CF).T,
        target_hot,
        precision=lax.Precision.HIGHEST,
        preferred_element_type=jnp.float32,
    )
    flux_register = (
        summed.reshape(5, CF * CF, 2, BOX_DEV)
        .transpose(0, 2, 1, 3)
        .reshape(5, 2 * CF * CF, BOX_DEV)
    )
    return (fine_next, flux_register)


def solution(mesh):
    in_specs = (
        P(None, "group", "dev"),
        P(("group", "dev"), None, None),
        P(("group", "dev"), None),
        P(("group", "dev")),
    )
    out_specs = (P(None, "group", "dev"), P(None, None, ("group", "dev")))
    return jax.shard_map(local, mesh=mesh, in_specs=in_specs, out_specs=out_specs, check_vma=False)
```

profile of v0, /device:TPU:1, one launch (start us, length us, event | category | flops | bytes accessed | tf_op | source)
XLA Modules:
  0.0 360.7 jit_solution(8431327879460411605)
XLA Ops:
  4.5 8.6 %all-to-all-start = ((s32[32,1,4]{2,1,0:T(1,128)}), s32[32,1,4]{2,1,0:T(1,128)S(1)}, u32[]{:S(2)}, u32[]{:S(2)}) async-start(s32[32,1,4]{2,1,0:T(1,128)} %bitcast.25), calls=%async_computation | async-start | bytes 32768 | tf_op jit(solution)/shard_map/all_to_all | solution.py:201
  13.1 4.6 %copy.1046 = f32[5,32,2048]{1,2,0:T(8,128)} copy(f32[5,32,2048]{2,1,0:T(8,128)} %param.4) | data formatting | bytes 2621440 | tf_op args[0]
  17.7 5.4 %copy.1047 = f32[5,32,128,16]{2,3,1,0:T(8,128)} copy(f32[5,32,128,16]{1,3,2,0:T(8,128)} %bitcast.232) | data formatting | bytes 2621440 | tf_op jit(solution)/shard_map/reshape | solution.py:171
  27.7 3.9 %collective-permute-start.3 = (f32[5,2,16,128]{3,2,1,0:T(8,128)}, f32[5,2,16,128]{3,2,1,0:T(8,128)S(1)}, u32[]{:S(2)}, u32[]{:S(2)}) collective-permute-start(f32[5,2,16,128]{3,2,1,0:T(8,128)} %get-tuple-element.143), channel_id=1, source_target_pairs={{32,0},{64,32},{96,64},{128,96},{160,128},{192,160},{224,192},{0,2... | collective-permute-start | bytes 245768 | tf_op jit(solution)/shard_map/ppermute | solution.py:30
  33.6 2.5 copy.1048
  36.1 3.8 %collective-permute-start = (f32[5,32,16,2]{1,2,3,0:T(8,128)}, f32[5,32,16,2]{1,2,3,0:T(8,128)}, u32[]{:S(2)}, u32[]{:S(2)}) collective-permute-start(f32[5,32,16,2]{1,2,3,0:T(8,128)} %copy.1048), channel_id=1, source_target_pairs={{0,1},{1,2},{2,3},{3,4},{4,5},{5,6},{6,7},{7,8},{8,9},{9,10},{10,1... | collective-permute-start | bytes 61448 | tf_op jit(solution)/shard_map/ppermute | solution.py:27
  41.8 2.4 collective-permute-start.1
  48.2 1.9 fusion.63
  50.1 2.0 fusion.65
  54.7 3.6 gather_fusion
  58.3 14.6 %reshape.2054 = f32[32,4,5,8,8,8]{5,4,3,1,0,2:T(8,128)} reshape(f32[128,5,512]{2,0,1:T(8,128)} %gather_fusion) | data formatting | bytes 2621440 | tf_op jit(solution)/shard_map/reshape | solution.py:127
  73.0 7.8 %fusion = f32[5,32,4,3,6,6]{5,4,3,2,1,0:T(8,128)S(1)} fusion(f32[32,4,5,8,8,8]{5,4,3,1,0,2:T(8,128)} %reshape.2054, pred[32,4]{1,0:T(8,128)(4,1)S(1)} %copy.1110), kind=kLoop, calls=%fused_computation.3 | loop fusion | flops 69120 | bytes 829568 | tf_op jit(solution)/shard_map/transpose | solution.py:138
  82.7 5.5 %select_select_fusion.1 = (f32[5,32,4,4,4]{4,3,2,1,0:T(4,128)S(1)}, f32[5,32,4,4,4]{4,3,2,1,0:T(4,128)}, f32[5,32,4,4,4]{4,3,2,1,0:T(4,128)}) fusion(f32[5,32,4,3,6,6]{5,4,3,2,1,0:T(8,128)S(1)} %fusion.3), kind=kLoop, calls=%fused_computation.58 | loop fusion | flops 276480 | bytes 409600 | tf_op jit(solution)/shard_map/jit(_where)/select_n | solution.py:36
  90.0 1.9 copy.1117
  91.9 1.9 copy.1114
  93.8 1.9 copy.1120
  99.3 2.9 select_bitcast_fusion
  102.3 11.0 %copy.1123 = f32[32,4,5,2,16,16]{5,4,3,1,2,0:T(8,128)} copy(f32[32,4,5,2,16,16]{0,5,4,3,1,2:T(8,128)} %select_bitcast_fusion) | data formatting | bytes 2621440 | tf_op jit(solution)/shard_map/jit(_where)/select_n | solution.py:206
  113.3 8.0 %reshape.2253 = f32[32,1,10240]{2,1,0:T(1,128)} reshape(f32[32,5,4,2,16,16]{5,4,3,2,1,0:T(8,128)} %bitcast.223) | data formatting | bytes 2621440
  121.3 7.7 %all-to-all-start.1 = ((f32[32,1,10240]{2,1,0:T(1,128)}), f32[32,1,10240]{2,1,0:T(1,128)}, u32[]{:S(2)}, u32[]{:S(2)}) async-start(f32[32,1,10240]{2,1,0:T(1,128)} %reshape.2253), calls=%async_computation.1 | async-start | bytes 2621440 | tf_op jit(solution)/shard_map/all_to_all | solution.py:209
  130.8 2.5 copy.1049
  133.3 2.5 maximum_select_fusion
  137.4 2.6 copy.1051
  142.5 3.8 %multiply_subtract_fusion.3 = (f32[5,32,16,128]{3,2,1,0:T(8,128)S(1)}, f32[5,32,16,128]{3,2,1,0:T(8,128)S(1)}, f32[5,32,16,128]{3,2,1,0:T(8,128)}) fusion(f32[5,32,16,128]{3,2,1,0:T(8,128)S(1)} %constant_dynamic-update-slice_fusion, f32[5,32,16,1]{3,2,1,0:T(8,128)S(1)} %bitcast.233, f32[5,32,16,127]{3,2,1,0:T(8,128)S(1)} %copy-done.14, ...), kind=kLoop, calls=%fused_computation.79 | loop fusion | flops 7536640 | bytes 9175040 | tf_op jit(solution)/shard_map/sub | solution.py:103
  146.3 2.1 fusion.10
  152.7 3.5 fusion.59
  172.5 2.2 constant_dynamic-update-slice_fusion.36
  207.2 2.5 add_divide_fusion.3
  214.6 5.1 %reduce.118 = f32[32,10240]{1,0:T(8,128)S(1)} reduce(f32[32,1,10240]{2,1,0:T(1,128)} %all-to-all-done.1, f32[]{:T(128)} %broadcast.1118), dimensions={1}, to_apply=%all_to_all.17.reduce_sub_computation | reduce | bytes 2621444 | tf_op jit(solution)/shard_map/all_to_all | solution.py:209
  219.7 5.8 %reshape.2254 = f32[32,5,4,2,16,16]{5,4,3,2,1,0:T(8,128)} reshape(f32[32,10240]{1,0:T(8,128)S(1)} %reduce.118) | data formatting | bytes 2621440
  225.5 9.9 %copy.1124 = f32[32,4,5,2,16,16]{5,4,3,2,1,0:T(8,128)} copy(f32[32,4,5,2,16,16]{5,4,3,1,2,0:T(8,128)} %bitcast.224) | data formatting | bytes 2621440 | tf_op jit(solution)/shard_map/all_to_all | solution.py:209
  235.4 6.4 %gather_fusion.1 = f32[32,5,2,16,16]{4,3,2,1,0:T(8,128)} fusion(f32[128,5,2,16,16]{4,3,2,1,0:T(8,128)} %bitcast.234, s32[1024]{0:T(1024)} %get-tuple-element.245), kind=kCustom, calls=%fused_computation.1 | custom fusion | bytes 655488 | tf_op jit(solution)/shard_map/gather | solution.py:211
  241.8 2.0 slice_bitcast_fusion.1
  243.8 1.9 copy.1159
  247.7 1.9 copy.1161
  251.6 5.6 %multiply_subtract_fusion = (f32[5,32,16,128]{3,2,1,0:T(8,128)S(1)}, f32[5,32,16,128]{3,2,1,0:T(8,128)S(1)}, f32[5,32,16,128]{3,2,1,0:T(8,128)S(1)}, f32[5,32,16...) fusion(f32[5,32,16,128]{3,2,1,0:T(8,128)S(1)} %constant_dynamic-update-slice_fusion, ...), kind=kLoop, calls=%fused_computation.51 | loop fusion | flops 15073280 | bytes 17039360 | tf_op jit(solution)/shard_map/sub | solution.py:103
  261.3 2.0 fusion.56
  263.3 2.1 fusion.45
  267.0 2.8 fusion.48
  277.1 2.2 stack.130
  293.9 2.2 stack.136
  312.5 1.9 constant_dynamic-update-slice_fusion.143
  323.4 3.9 %fusion.1 = f32[5,2,4,8,4]{4,3,2,1,0:T(8,128)S(1)} fusion(f32[5,2,1,4,4,8,1,4,4]{8,7,5,4,3,1,6,2,0:T(4,128)S(1)} %constant_dynamic-update-slice_fusion.135, f32[5,2,1,4,4,8,1,4,4]{8,7,5,4,3,1,6,2,0:T(4,128)S(1)} %constant_dynamic-update-slice_fusion.140, f32[5,2,1,4,4,8,1,4,4]{8,7,5,4,3,1,6,2,0:T(4,128)S(1)} %constant_dynamic-update-slice_fusion.130, ...), kind=kLoop, calls=%fused_computation.6 | loop fusion | flops 162560 | bytes 398336 | tf_op jit(solution)/shard_map/reduce_sum | solution.py:161
  327.3 4.9 %reshape_squeeze.4 = f32[5,2,4,4,8,4,4]{6,5,4,3,2,1,0:T(4,128)} reshape(f32[5,32,128]{2,1,0:T(8,128)S(1)} %slice_reduce_fusion) | data formatting | bytes 163840 | tf_op jit(solution)/shard_map/reshape;squeeze | solution.py:160
  332.2 2.4 reduce_sum.41
  336.1 7.4 %all-to-all-start.2 = ((f32[32,4,80]{2,1,0:T(4,128)}), f32[32,4,80]{2,1,0:T(4,128)S(1)}, u32[]{:S(2)}, u32[]{:S(2)}) async-start(f32[32,4,80]{2,1,0:T(4,128)} %copy.1151), calls=%async_computation.2 | async-start | bytes 131072 | tf_op jit(solution)/shard_map/all_to_all | solution.py:226
  350.3 4.1 %copy.1149 = f32[5,32,128,16]{1,3,2,0:T(8,128)} copy(f32[5,32,128,16]{2,3,1,0:T(8,128)S(1)} %fusion.15) | data formatting | bytes 2621440 | tf_op jit(solution)/shard_map/transpose | solution.py:216
  354.4 5.0 %copy.1153 = f32[5,32,2048]{2,1,0:T(8,128)} copy(f32[5,32,2048]{1,2,0:T(8,128)} %bitcast.231) | data formatting | bytes 2621440
  (420 shorter events, 154.7 us)
Async XLA Ops:
  0.6 54.1 %copy-start = (f32[128,5,512]{2,0,1:T(8,128)S(1)}, f32[128,5,512]{2,0,1:T(8,128)}, u32[]{:S(2)}) copy-start(f32[128,5,512]{2,0,1:T(8,128)} %param.5) | copy-start | bytes 3932164
  3.0 14.6 %copy-start.79 = (s32[32]{0:T(128)}, s32[32]{0:T(128)S(1)}, u32[]{:S(2)}) copy-start(s32[32]{0:T(128)S(1)} %get-tuple-element.235) | copy-start | bytes 388
  4.5 49.3 %all-to-all-start = ((s32[32,1,4]{2,1,0:T(1,128)}), s32[32,1,4]{2,1,0:T(1,128)S(1)}, u32[]{:S(2)}, u32[]{:S(2)}) async-start(s32[32,1,4]{2,1,0:T(1,128)} %bitcast.25), calls=%async_computation | async-start | bytes 32768 | tf_op jit(solution)/shard_map/all_to_all | solution.py:201
  23.1 2.2 copy-start.4
  26.1 187.2 %collective-permute-start.2 = (f32[5,2,16,128]{3,2,1,0:T(8,128)}, f32[5,2,16,128]{3,2,1,0:T(8,128)}, u32[]{:S(2)}, u32[]{:S(2)}) collective-permute-start(f32[5,2,16,128]{3,2,1,0:T(8,128)} %get-tuple-element.142), channel_id=1, source_target_pairs={{0,32},{32,64},{64,96},{96,128},{128,160},{160,192},{192,224},{224... | collective-permute-start | bytes 245768 | tf_op jit(solution)/shard_map/ppermute | solution.py:27
  27.7 186.3 %collective-permute-start.3 = (f32[5,2,16,128]{3,2,1,0:T(8,128)}, f32[5,2,16,128]{3,2,1,0:T(8,128)S(1)}, u32[]{:S(2)}, u32[]{:S(2)}) collective-permute-start(f32[5,2,16,128]{3,2,1,0:T(8,128)} %get-tuple-element.143), channel_id=1, source_target_pairs={{32,0},{64,32},{96,64},{128,96},{160,128},{192,160},{224,192},{0,2... | collective-permute-start | bytes 245768 | tf_op jit(solution)/shard_map/ppermute | solution.py:30
  36.1 94.7 %collective-permute-start = (f32[5,32,16,2]{1,2,3,0:T(8,128)}, f32[5,32,16,2]{1,2,3,0:T(8,128)}, u32[]{:S(2)}, u32[]{:S(2)}) collective-permute-start(f32[5,32,16,2]{1,2,3,0:T(8,128)} %copy.1048), channel_id=1, source_target_pairs={{0,1},{1,2},{2,3},{3,4},{4,5},{5,6},{6,7},{7,8},{8,9},{9,10},{10,1... | collective-permute-start | bytes 61448 | tf_op jit(solution)/shard_map/ppermute | solution.py:27
  41.8 95.5 %collective-permute-start.1 = (f32[5,32,16,2]{1,2,3,0:T(8,128)S(1)}, f32[5,32,16,2]{1,2,3,0:T(8,128)}, u32[]{:S(2)}, u32[]{:S(2)}) collective-permute-start(f32[5,32,16,2]{1,2,3,0:T(8,128)S(1)} %copy.1050), channel_id=1, source_target_pairs={{1,0},{2,1},{3,2},{4,3},{5,4},{6,5},{7,6},{8,7},{9,8},{10,9},{11,1... | collective-permute-start | bytes 61448 | tf_op jit(solution)/shard_map/ppermute | solution.py:30
  121.3 92.7 %all-to-all-start.1 = ((f32[32,1,10240]{2,1,0:T(1,128)}), f32[32,1,10240]{2,1,0:T(1,128)}, u32[]{:S(2)}, u32[]{:S(2)}) async-start(f32[32,1,10240]{2,1,0:T(1,128)} %reshape.2253), calls=%async_computation.1 | async-start | bytes 2621440 | tf_op jit(solution)/shard_map/all_to_all | solution.py:209
  137.4 2.6 copy-start.15
  140.0 2.1 copy-start.13
  140.0 2.5 copy-start.14
  194.3 3.2 copy-start.46
  201.8 5.2 %copy-start.21 = (f32[1,32,16,128]{3,2,1,0:T(8,128)S(1)}, f32[1,32,16,128]{3,2,1,0:T(8,128)}, u32[]{:S(2)}) copy-start(f32[1,32,16,128]{3,2,1,0:T(8,128)} %get-tuple-element.102) | copy-start | bytes 786436
  203.6 3.5 copy-start.47
  207.1 2.6 copy-start.74
  207.1 2.6 copy-start.75
  207.1 2.6 copy-start.76
  209.7 3.5 copy-start.10
  214.1 5.6 %copy-start.48 = (f32[5,2,16,128]{3,2,1,0:T(8,128)}, f32[5,2,16,128]{3,2,1,0:T(8,128)S(1)}, u32[]{:S(2)}) copy-start(f32[5,2,16,128]{3,2,1,0:T(8,128)S(1)} %collective-permute-done.3) | copy-start | bytes 245764
  266.1 3.7 %copy-start.60 = (f32[1,32,1,128]{3,2,1,0:T(1,128)S(1)}, f32[1,32,1,128]{3,2,1,0:T(1,128)}, u32[]{:S(2)}) copy-start(f32[1,32,1,128]{3,2,1,0:T(1,128)} %get-tuple-element.199) | copy-start | bytes 49156
  269.8 9.5 %copy-start.58 = (f32[32,128]{1,0:T(8,128)S(1)}, f32[32,128]{1,0:T(8,128)}, u32[]{:S(2)}) copy-start(f32[32,128]{1,0:T(8,128)} %get-tuple-element.194) | copy-start | bytes 49156
  270.5 10.2 %copy-start.57 = (f32[32,128]{1,0:T(8,128)S(1)}, f32[32,128]{1,0:T(8,128)}, u32[]{:S(2)}) copy-start(f32[32,128]{1,0:T(8,128)} %get-tuple-element.191) | copy-start | bytes 49156
  273.5 8.8 %copy-start.59 = (f32[32,128]{1,0:T(8,128)S(1)}, f32[32,128]{1,0:T(8,128)}, u32[]{:S(2)}) copy-start(f32[32,128]{1,0:T(8,128)} %get-tuple-element.184) | copy-start | bytes 49156
  276.4 7.4 %copy-start.70 = (f32[32,128]{1,0:T(8,128)S(1)}, f32[32,128]{1,0:T(8,128)}, u32[]{:S(2)}) copy-start(f32[32,128]{1,0:T(8,128)} %get-tuple-element.181) | copy-start | bytes 49156
  280.8 6.4 %copy-start.69 = (f32[1,32,1,128]{3,2,1,0:T(1,128)S(1)}, f32[1,32,1,128]{3,2,1,0:T(1,128)}, u32[]{:S(2)}) copy-start(f32[1,32,1,128]{3,2,1,0:T(1,128)} %get-tuple-element.205) | copy-start | bytes 49156
  282.3 7.1 %copy-start.68 = (f32[1,32,1,128]{3,2,1,0:T(1,128)S(1)}, f32[1,32,1,128]{3,2,1,0:T(1,128)}, u32[]{:S(2)}) copy-start(f32[1,32,1,128]{3,2,1,0:T(1,128)} %get-tuple-element.202) | copy-start | bytes 49156
  287.1 9.0 %copy-start.67 = (f32[32,128]{1,0:T(8,128)S(1)}, f32[32,128]{1,0:T(8,128)}, u32[]{:S(2)}) copy-start(f32[32,128]{1,0:T(8,128)} %get-tuple-element.200) | copy-start | bytes 49156
  287.9 9.7 %copy-start.66 = (f32[32,128]{1,0:T(8,128)S(1)}, f32[32,128]{1,0:T(8,128)}, u32[]{:S(2)}) copy-start(f32[32,128]{1,0:T(8,128)} %get-tuple-element.47) | copy-start | bytes 49156
  290.1 9.0 %copy-start.56 = (f32[32,128]{1,0:T(8,128)S(1)}, f32[32,128]{1,0:T(8,128)}, u32[]{:S(2)}) copy-start(f32[32,128]{1,0:T(8,128)} %get-tuple-element.187) | copy-start | bytes 49156
  292.3 8.3 %copy-start.51 = (f32[5,32,1,128]{3,2,1,0:T(1,128)S(1)}, f32[5,32,1,128]{3,2,1,0:T(1,128)}, u32[]{:S(2)}) copy-start(f32[5,32,1,128]{3,2,1,0:T(1,128)} %copy-done.50) | copy-start | bytes 245764
  292.4 8.3 %copy-start.55 = (f32[1,32,1,128]{3,2,1,0:T(1,128)S(1)}, f32[1,32,1,128]{3,2,1,0:T(1,128)}, u32[]{:S(2)}) copy-start(f32[1,32,1,128]{3,2,1,0:T(1,128)} %get-tuple-element.186) | copy-start | bytes 49156
  300.6 8.7 %copy-start.54 = (f32[32,128]{1,0:T(8,128)S(1)}, f32[32,128]{1,0:T(8,128)}, u32[]{:S(2)}) copy-start(f32[32,128]{1,0:T(8,128)} %get-tuple-element.26) | copy-start | bytes 49156
  301.3 9.7 %copy-start.53 = (f32[32,128]{1,0:T(8,128)S(1)}, f32[32,128]{1,0:T(8,128)}, u32[]{:S(2)}) copy-start(f32[32,128]{1,0:T(8,128)} %get-tuple-element.22) | copy-start | bytes 49156
  316.5 2.2 copy-start.20
  319.8 3.1 copy-start.39
  336.1 23.3 %all-to-all-start.2 = ((f32[32,4,80]{2,1,0:T(4,128)}), f32[32,4,80]{2,1,0:T(4,128)S(1)}, u32[]{:S(2)}, u32[]{:S(2)}) async-start(f32[32,4,80]{2,1,0:T(4,128)} %copy.1151), calls=%async_computation.2 | async-start | bytes 131072 | tf_op jit(solution)/shard_map/all_to_all | solution.py:226
  345.8 2.9 copy-start.16
  345.8 2.9 copy-start.17
  345.8 2.9 copy-start.18
  346.3 2.0 copy-start.64
  346.3 2.4 copy-start.7
  346.3 2.6 copy-start.11
  346.5 2.1 copy-start.52
  346.5 2.9 copy-start.5
  354.4 5.1 %copy-start.78 = (s32[128]{0:T(128)S(1)}, s32[128]{0:T(128)}, u32[]{:S(2)}) copy-start(s32[128]{0:T(128)} %eq.124) | copy-start | bytes 1540
  354.4 5.1 %copy-start.81 = (s32[2,128]{1,0:T(2,128)S(1)}, s32[2,128]{1,0:T(2,128)}, u32[]{:S(2)}) copy-start(s32[2,128]{1,0:T(2,128)} %multiply_add_fusion.19) | copy-start | bytes 3076
  354.4 6.0 %copy-start.1 = (f32[128,5,512]{2,0,1:T(8,128)S(1)}, f32[128,5,512]{2,0,1:T(8,128)}, u32[]{:S(2)}) copy-start(f32[128,5,512]{2,0,1:T(8,128)} %param.5) | copy-start | bytes 3932164
  (42 other events, 62.1 us)
where the time goes:
time: 368 us; the launch traced here: 361 us
  local copies, waits for them, and re-layouts  231 us (63%)
  other arithmetic  90.8 us (25%)
  starting transfers between devices  35.5 us (10%)
    unnamed x200, local copies, waits for them, and re-layouts  54.4 us
    another operation x20, local copies, waits for them, and re-layouts, state_terms(): jnp.stack(cons_list)  16.5 us
    another operation x14, local copies, waits for them, and re-layouts, state_terms(): jnp.stack(flux_list)  15.8 us
    unnamed x52, other arithmetic  14.7 us
    reshape x1, local copies, waits for them, and re-layouts, extract(): shaped = box_cells.reshape(box_cells.shape[:-1] + (CB, CB, CB))  14.6 us
    slice x13, local copies, waits for them, and re-layouts, part_of(): return lax.slice_in_dim(array, start, stop, axis=dim_index)  11.8 us
    select_n x1, local copies, waits for them, and re-layouts, local(): jnp.where(slot_live[..., None, None, None, None], interpolate(coarse_cut,...  11 us
    all_to_all x2, local copies, waits for them, and re-layouts, local(): lax.all_to_all(payload, 'dev', split_axis=0, concat_axis=0, tiled=True)  10.4 us
  transfers between devices with their start and end apart: 7, of which 0 were waited for; matrix products, arithmetic and copies ran while one was open for 52% of the time, Pallas kernels for 0%

commit v1 on v0

v1 whole, which is shorter than its diff:
```python
import functools

import jax
import jax.numpy as jnp
from jax import lax
from jax.experimental import pallas as pl
from jax.experimental.pallas import tpu as pltpu
from jax.sharding import PartitionSpec as P

BOX_DEV = 128
PIECES_DEV = 32
MOST = 4
GAMMA = 1.4
DT_DX = 0.08
TILES = 16
ROWS = 32
LANES = 128
MESH = pl.DeviceIdType.MESH
F32 = jnp.float32
BF16 = jnp.bfloat16


def iota(shape, axis):
    return lax.broadcasted_iota(jnp.int32, shape, axis)


def minmod(a, b):
    return jnp.maximum(jnp.minimum(a, b), jnp.minimum(jnp.maximum(a, b), 0.0))


def primitives(q):
    r = 1.0 / q[0]
    u, v, w = q[1] * r, q[2] * r, q[3] * r
    p = (GAMMA - 1.0) * (q[4] - 0.5 * (q[1] * u + q[2] * v + q[3] * w))
    return [q[0], u, v, w, p]


def hll(low, up, normal):
    n = 1 + normal
    t1, t2 = [i for i in (1, 2, 3) if i != n]
    rl, ul, pl_ = low[0], low[n], low[4]
    ru, uu, pu = up[0], up[n], up[4]
    ql, qu = GAMMA * pl_, GAMMA * pu
    cl = ql * lax.rsqrt(ql * rl)
    cu = qu * lax.rsqrt(qu * ru)
    slow = jnp.minimum(jnp.minimum(ul - cl, uu - cu), 0.0)
    fast = jnp.maximum(jnp.maximum(ul + cl, uu + cu), 0.0)
    inverse = 1.0 / (fast - slow)
    a = fast * inverse
    b = slow * inverse
    e = slow * a
    aul = a * ul
    buu = b * uu
    wl = aul - e
    wu = e - buu
    ml = rl * wl
    mu = ru * wu
    nl, nu = ml * ul, mu * uu
    v1l, v1u = ml * low[t1], mu * up[t1]
    v2l, v2u = ml * low[t2], mu * up[t2]
    kinetic = (nl * ul + v1l * low[t1] + v2l * low[t2]) + (nu * uu + v1u * up[t1] + v2u * up[t2])
    flux = [None] * 5
    flux[0] = ml + mu
    flux[n] = (nl + nu) + (a * pl_ - b * pu)
    flux[t1] = v1l + v1u
    flux[t2] = v2l + v2u
    flux[4] = 0.5 * kinetic + (pl_ * (2.5 * wl + aul) + pu * (2.5 * wu - buu))
    return flux


def face(before_two, before, here, after, normal):
    low, up = [], []
    for f in range(5):
        d1 = here[f] - before[f]
        low.append(before[f] + 0.5 * minmod(before[f] - before_two[f], d1))
        up.append(here[f] - 0.5 * minmod(d1, after[f] - here[f]))
    return hll(low, up, normal)


def swap_tiles(tiles):
    tiles = list(tiles)
    lane = iota(tiles[0].shape, 1)
    for bit in range(4):
        step = 1 << bit
        odd = (lane & step) != 0
        for t in range(16):
            if t & step:
                continue
            a, b = tiles[t], tiles[t + step]
            tiles[t] = jnp.where(odd, pltpu.roll(b, step, 1), a)
            tiles[t + step] = jnp.where(odd, b, pltpu.roll(a, LANES - step, 1))
    return tiles


def parts(x):
    first = x.astype(BF16)
    rest = x - first.astype(F32)
    second = rest.astype(BF16)
    third = (rest - second.astype(F32)).astype(BF16)
    return first, second, third


def kernel(
    members, groups,
    fine, boxes, owner_in, box_in,
    out, register,
    q_s, w_s, p_s, fx_s, fy_s, ft_s, fz_s, o_s, cb_s, u_s, ids_s,
    ask_s, asked_s, give_s, got_s, sum_s, sums_s, ex_s, se_s, xh_s, yh_s, reg_s,
    load_sem, out_sem, ask_send, ask_recv, give_send, give_recv, sum_send, sum_recv, halo_send, halo_recv,
):
    me = lax.axis_index("dev")
    group = lax.axis_index("group")

    load_ids = [
        pltpu.make_async_copy(owner_in, ids_s.at[0:1], load_sem.at[0]),
        pltpu.make_async_copy(box_in, ids_s.at[1:2], load_sem.at[1]),
    ]
    load_boxes = pltpu.make_async_copy(boxes, cb_s, load_sem.at[2])
    load_fine = pltpu.make_async_copy(fine, q_s, load_sem.at[3])
    for copy in load_ids:
        copy.start()
    load_boxes.start()
    load_fine.start()

    barrier = pltpu.get_barrier_semaphore()
    north, south = lax.rem(group + 1, groups), lax.rem(group + groups - 1, groups)

    def greet(k, c):
        pl.semaphore_signal(
            barrier, inc=1, device_id=(group, lax.rem(me + k, members)), device_id_type=MESH
        )
        return c

    for y in (north, south):
        pl.semaphore_signal(barrier, inc=1, device_id=(y, me), device_id_type=MESH)
    lax.fori_loop(1, members, greet, 0)

    lane1 = iota((1, LANES), 1)
    row128 = iota((LANES, LANES), 0)
    lane128 = iota((LANES, LANES), 1)
    lane8 = iota((8, LANES), 1)
    row8 = iota((8, LANES), 0)

    for copy in load_ids:
        copy.wait()
    live = lane1 < PIECES_DEV
    owner = jnp.where(live, ids_s[0:1, :], -1)
    box = ids_s[1:2, :]
    row32, lane32 = iota((PIECES_DEV, LANES), 0), iota((PIECES_DEV, LANES), 1)
    owner_f = owner.astype(F32)
    owner_all = jnp.broadcast_to(owner_f, (PIECES_DEV, LANES))
    owner_col = jnp.sum(jnp.where(lane32 == row32, owner_all, 0.0), axis=1, keepdims=True)
    same = (jnp.broadcast_to(owner_col, (PIECES_DEV, LANES)) == owner_all) & (row32 < lane32)
    rank = jnp.sum(jnp.where(same, 1.0, 0.0), axis=0, keepdims=True)
    away = owner - me
    away = jnp.where(away < 0, away + members, away)
    slot = jnp.where(live, MOST * away + rank.astype(jnp.int32), -1)
    value = (box + 1 + BOX_DEV * (lane1 & 1)).astype(F32)
    hit = row128 == jnp.broadcast_to(slot, (LANES, LANES))
    asked_value = jnp.sum(
        jnp.where(hit, jnp.broadcast_to(value, (LANES, LANES)), 0.0), axis=1, keepdims=True
    )
    ask_s[...] = jnp.broadcast_to(asked_value, (LANES, LANES))

    pl.semaphore_wait(barrier, members + 1)

    def exchange(buffer, landed, send, recv, sign, part):
        def copy(k):
            return pltpu.make_async_remote_copy(
                src_ref=part(buffer, k),
                dst_ref=part(landed, k),
                send_sem=send,
                recv_sem=recv,
                device_id=(group, lax.rem(me + sign * k + members, members)),
                device_id_type=MESH,
            )

        def start(k, c):
            copy(k).start()
            return c

        lax.fori_loop(1, members, start, 0)

    def all_of(landed, send, recv, part):
        whole = part(landed)
        return pltpu.make_async_remote_copy(
            src_ref=whole, dst_ref=whole, send_sem=send, recv_sem=recv,
            device_id=(group, lax.rem(me + 1, members)), device_id_type=MESH,
        )

    one = lambda ref, k: ref.at[pl.ds(k * MOST, MOST)]
    one3 = lambda ref, k: ref.at[:, pl.ds(k * MOST, MOST)]
    rest = lambda ref: ref.at[pl.ds(MOST, (members - 1) * MOST)]
    rest3 = lambda ref: ref.at[:, pl.ds(MOST, (members - 1) * MOST)]

    exchange(ask_s, asked_s, ask_send, ask_recv, 1, one)
    asked_s[0:MOST, :] = ask_s[0:MOST, :]

    right, left = lax.rem(me + 1, members), lax.rem(me + members - 1, members)
    last = fine.shape[2] - LANES
    halos = [
        (fine.at[:, :, pl.ds(last, LANES)], xh_s.at[0], (group, right)),
        (fine.at[:, :, pl.ds(0, LANES)], xh_s.at[1], (group, left)),
        (fine.at[:, pl.ds(ROWS - 2, 2)], yh_s.at[0], (north, me)),
        (fine.at[:, pl.ds(0, 2)], yh_s.at[1], (south, me)),
    ]
    halo_copies = [
        pltpu.make_async_remote_copy(
            src_ref=src, dst_ref=dst, send_sem=halo_send.at[i], recv_sem=halo_recv.at[i],
            device_id=target, device_id_type=MESH,
        )
        for i, (src, dst, target) in enumerate(halos)
    ]
    for copy in halo_copies:
        copy.start()

    spots = []
    for ky in range(2):
        v = slot if ky == 0 else pltpu.roll(slot, LANES - 16, 1)
        v = jnp.where(lane1 < 16, v, 0)
        for step in (16, 32, 64):
            v = v + pltpu.roll(v, step, 1)
        odd = (lane1 & 1) != 0
        spots.append(jnp.where(odd, pltpu.roll(v, 1, 1), v))
        spots.append(jnp.where(odd, v, pltpu.roll(v, LANES - 1, 1)))
    spot = jnp.concatenate(
        [
            jnp.where(row128 == jnp.broadcast_to(s, (LANES, LANES)), 1.0, 0.0).astype(BF16)
            for s in spots
        ],
        axis=1,
    )

    load_boxes.wait()

    def table(n, c):
        rows = pl.ds(pl.multiple_of(n * 16, 16), 16)
        lane = iota((16, LANES), 1)
        lo = lane < 64
        t = [[cb_s[f, rows, k * LANES : (k + 1) * LANES] for k in range(4)] for f in range(5)]
        mid = primitives([jnp.where(lo, t[f][1], t[f][2]) for f in range(5)])
        below = primitives([jnp.where(lo, t[f][2], t[f][0]) for f in range(5)])
        above = primitives([jnp.where(lo, t[f][3], t[f][1]) for f in range(5)])
        first_y, first_x = (lane & 32) == 0, (lane & 4) == 0
        packed = []
        for f in range(5):
            m = mid[f]
            sz = minmod(m - pltpu.roll(below[f], 64, 1), pltpu.roll(above[f], 64, 1) - m)
            sy = minmod(m - pltpu.roll(m, 8, 1), pltpu.roll(m, LANES - 8, 1) - m)
            sx = minmod(m - pltpu.roll(m, 1, 1), pltpu.roll(m, LANES - 1, 1) - m)
            packed.append(
                jnp.where(
                    first_y,
                    jnp.where(first_x, pltpu.roll(m, LANES - 18, 1), pltpu.roll(sz, LANES - 14, 1)),
                    jnp.where(first_x, pltpu.roll(sy, 14, 1), pltpu.roll(sx, 18, 1)),
                )
            )
        cx, h, coef, cy = lane >> 5, (lane >> 4) & 1, (lane >> 2) & 3, lane & 3
        source = h * 64 + (coef >> 1) * 32 + cy * 8 + (coef & 1) * 4 + cx
        for pair in range(3):
            a = packed[2 * pair]
            b = packed[2 * pair + 1] if pair < 2 else a
            for side, tile in (
                (0, jnp.where(lo, pltpu.roll(a, 64, 1), b)),
                (1, jnp.where(lo, a, pltpu.roll(b, 64, 1))),
            ):
                moved = jnp.take_along_axis(tile, source, axis=1)
                where = pl.ds(pl.multiple_of(side * BOX_DEV + n * 16, 16), 16)
                for i, x in enumerate(parts(moved)):
                    u_s[i, where, pair * LANES : (pair + 1) * LANES] = x
        return c

    lax.fori_loop(0, BOX_DEV // 16, table, 0)

    load_fine.wait()

    def to_primitive(t, c):
        lanes = pl.ds(pl.multiple_of(t * LANES, LANES), LANES)
        w = primitives([q_s[f, :, lanes] for f in range(5)])
        for f in range(5):
            w_s[f, t + 1, 8 : 8 + ROWS, :] = w[f]
        return c

    lax.fori_loop(0, TILES, to_primitive, 0)

    all_of(asked_s, ask_send, ask_recv, rest).wait()
    asked = asked_s[...]
    lane_f = lane128.astype(F32)
    chosen = jnp.concatenate(
        [
            jnp.where(asked == lane_f + (1.0 + BOX_DEV * side), 1.0, 0.0).astype(BF16)
            for side in range(2)
        ],
        axis=1,
    )

    def dot(a, b, da, db):
        return lax.dot_general(a, b, (((da,), (db,)), ((), ())), preferred_element_type=F32)

    give = sum(dot(chosen, u_s[i], 1, 0) for i in range(3))
    for pair in range(3):
        give_s[pair] = give[:, pair * LANES : (pair + 1) * LANES]
    exchange(give_s, got_s, give_send, give_recv, -1, one3)
    got_s[:, 0:MOST, :] = give_s[:, 0:MOST, :]

    def pack(n, c):
        f, rb = n // 4, n % 4
        rows = pl.ds(pl.multiple_of(8 + rb * 8, 8), 8)
        tiles = swap_tiles([w_s[f, 1 + t, rows, :] for t in range(TILES)])
        for z in range(16):
            p_s[f, 2 + z, pl.ds(pl.multiple_of(rb * 8, 8), 8), :] = tiles[z]
        return c

    lax.fori_loop(0, 20, pack, 0)

    def z_face(k, half):
        rows = slice(16 * half, 16 * half + 16)
        w = [[p_s[f, k + i, rows, :] for f in range(5)] for i in range(4)]
        flux = face(*w, 2)
        for f in range(5):
            fz_s[f, k, rows, :] = flux[f]

    def z_inner(k, c):
        z_face(k, 0)
        z_face(k, 1)
        return c

    lax.fori_loop(2, 15, z_inner, 0)

    for copy in halo_copies:
        copy.wait()
    lane_r = iota((ROWS, LANES), 1)
    x_low = primitives([xh_s[0, f] for f in range(5)])
    x_high = primitives([xh_s[1, f] for f in range(5)])
    is_first = jnp.full((ROWS, LANES), me, jnp.int32) == 0
    is_last = jnp.full((ROWS, LANES), me, jnp.int32) == members - 1
    inner = slice(8, 8 + ROWS)
    for f in range(5):
        begin, end = w_s[f, 1, inner, :], w_s[f, TILES, inner, :]
        low_edge = jnp.where(lane_r < 112, pltpu.roll(begin, 96, 1), pltpu.roll(begin, 112, 1))
        high_edge = jnp.where(lane_r < 16, pltpu.roll(end, 16, 1), pltpu.roll(end, 32, 1))
        w_s[f, 0, inner, :] = jnp.where(is_first, low_edge, x_low[f])
        w_s[f, TILES + 1, inner, :] = jnp.where(is_last, high_edge, x_high[f])

    def y_halo(t, c):
        lanes = pl.ds(pl.multiple_of(t * LANES, LANES), LANES)
        low = primitives([yh_s[0, f, :, lanes] for f in range(5)])
        high = primitives([yh_s[1, f, :, lanes] for f in range(5)])
        for f in range(5):
            w_s[f, t + 1, 6:8, :] = low[f]
            w_s[f, t + 1, 8 + ROWS : 10 + ROWS, :] = high[f]
        return c

    lax.fori_loop(0, TILES, y_halo, 0)

    lane_h = iota((16, LANES), 1)

    def x_faces(t, c):
        after_tile = jnp.minimum(t + 1, TILES + 1)
        for half in range(2):
            rows = slice(8 + 16 * half, 24 + 16 * half)
            w = [[], [], [], []]
            for f in range(5):
                left_tile, tile, right_tile = w_s[f, t - 1, rows, :], w_s[f, t, rows, :], w_s[f, after_tile, rows, :]
                w[0].append(pltpu.roll(jnp.where(lane_h >= 96, left_tile, tile), 32, 1))
                w[1].append(pltpu.roll(jnp.where(lane_h >= 112, left_tile, tile), 16, 1))
                w[2].append(tile)
                w[3].append(pltpu.roll(jnp.where(lane_h < 16, right_tile, tile), LANES - 16, 1))
            flux = face(*w, 0)
            for f in range(5):
                fx_s[f, t, 16 * half : 16 * half + 16, :] = flux[f]
        return c

    lax.fori_loop(1, TILES + 2, x_faces, 0)

    top = face(*[[w_s[f, 1 : 1 + TILES, 38 + i, :] for f in range(5)] for i in range(4)], 1)
    for f in range(5):
        ft_s[f] = top[f]

    def y_faces(t, c):
        lanes = pl.ds(pl.multiple_of(t * LANES, LANES), LANES)
        for half in range(2):
            first = 6 + 16 * half
            w = [[w_s[f, t + 1, first + i : first + i + 16, :] for f in range(5)] for i in range(4)]
            flux = face(*w, 1)
            for f in range(5):
                fy_s[f, 16 * half : 16 * half + 16, :] = flux[f]
        for f in range(5):
            fy_s[f, ROWS : ROWS + 1, :] = ft_s[f, pl.ds(t, 1), :]
        for f in range(5):
            low, high = fx_s[f, t + 1], fx_s[f, t + 2]
            dx = pltpu.roll(jnp.where(lane_r < 16, high, low), LANES - 16, 1) - low
            dy = fy_s[f, 1 : 1 + ROWS, :] - fy_s[f, 0:ROWS, :]
            o_s[f, :, lanes] = q_s[f, :, lanes] - DT_DX * (dx + dy)
        return c

    lax.fori_loop(0, TILES, y_faces, 0)

    all_of(got_s, give_send, give_recv, rest3).wait()
    for pair in range(3):
        got = parts(got_s[pair])
        ex_s[pair] = sum(dot(x, spot, 0, 0) for x in got)
    t8, i8 = lane8 & 15, lane8 >> 4
    cx8 = 2 * (t8 & 1) + (i8 >> 2)
    ix_offset = ((i8 & 3).astype(F32) + 0.5) * 0.25 - 0.5
    iy_offset = ((row8 & 3).astype(F32) + 0.5) * 0.25 - 0.5
    cx32 = 2 * (lane_r & 1) + (lane_r >> 6)
    for pair in range(3):
        for kys in range(4):
            lanes = slice(kys * LANES, (kys + 1) * LANES)
            x = [ex_s[pair, 32 * cx : 32 * cx + 32, lanes] for cx in range(4)]
            se_s[pair, kys] = jnp.where(
                cx32 < 2, jnp.where(cx32 == 0, x[0], x[1]), jnp.where(cx32 == 2, x[2], x[3])
            )
    for f in range(5):
        pair, h = f // 2, f % 2
        for ky in range(2):
            for s in range(2):
                kys = 2 * ky + s
                for hh in range(2):
                    def coefficient(q):
                        r = h * 16 + q * 4 + 2 * hh
                        return jnp.where(
                            row8 < 4,
                            jnp.broadcast_to(se_s[pair, kys, r : r + 1, :], (8, LANES)),
                            jnp.broadcast_to(se_s[pair, kys, r + 1 : r + 2, :], (8, LANES)),
                        )

                    centre, slope_z = coefficient(0), coefficient(1)
                    slope_y, slope_x = coefficient(2), coefficient(3)
                    rows = slice(ky * 16 + hh * 8, ky * 16 + hh * 8 + 8)
                    for layer in range(2):
                        oz = (0.125, 0.375)[layer] if s == 0 else (-0.375, -0.125)[layer]
                        plane = layer if s == 0 else 18 + layer
                        p_s[f, plane, rows, :] = (
                            (centre + slope_z * oz) + slope_y * iy_offset
                        ) + slope_x * ix_offset

    for k in (0, 16):
        z_face(k, 0)
        z_face(k, 1)

    row_f = iota((ROWS, LANES), 0)
    keep = jnp.where(cx32 == (row_f & 3), 0.25, 0.0)
    odd1, odd2 = (row_f & 1) != 0, (row_f & 2) != 0
    terms = [[[] for _ in range(2)] for _ in range(2)]
    for s in range(2):
        for f in range(5):
            x = fz_s[f, 16 * s]
            x = x + jnp.where(odd1, pltpu.roll(x, 1, 0), pltpu.roll(x, ROWS - 1, 0))
            x = x + jnp.where(odd2, pltpu.roll(x, 2, 0), pltpu.roll(x, ROWS - 2, 0))
            x = x * keep
            terms[0][s].append(x[0:16])
            terms[1][s].append(x[16:32])
    pad = jnp.zeros((48, LANES), F32)
    all_terms = jnp.concatenate(
        [jnp.concatenate(terms[ky][s] + [pad], axis=0) for ky in range(2) for s in range(2)], axis=1
    )
    sum_s[...] = sum(dot(spot, x, 1, 1) for x in parts(all_terms))
    exchange(sum_s, sums_s, sum_send, sum_recv, 1, one)
    sums_s[0:MOST, :] = sum_s[0:MOST, :]

    for k in (1, 15):
        z_face(k, 0)
        z_face(k, 1)

    def finish(n, c):
        f, rb = n // 4, n % 4
        rows = pl.ds(pl.multiple_of(rb * 8, 8), 8)
        z = [fz_s[f, k, rows, :] for k in range(17)]
        tiles = swap_tiles([z[k + 1] - z[k] for k in range(16)])
        for t in range(TILES):
            lanes = slice(t * LANES, (t + 1) * LANES)
            o_s[f, rows, lanes] = o_s[f, rows, lanes] - DT_DX * tiles[t]
        return c

    lax.fori_loop(0, 20, finish, 0)
    store = pltpu.make_async_copy(o_s, out, out_sem.at[0])
    store.start()

    all_of(sums_s, sum_send, sum_recv, rest).wait()
    total = sum(dot(x, chosen, 0, 0) for x in parts(sums_s[...]))
    for f in range(5):
        for s in range(2):
            reg_s[f, 16 * s : 16 * s + 16, :] = total[
                16 * f : 16 * f + 16, s * LANES : (s + 1) * LANES
            ]
    store_register = pltpu.make_async_copy(reg_s, register, out_sem.at[1])
    store_register.start()
    store.wait()
    store_register.wait()


def local(fine_state, coarse_boxes, piece_owner, piece_box):
    members, groups = lax.axis_size("dev"), lax.axis_size("group")
    boxes = coarse_boxes.transpose(1, 0, 2)
    owner = jnp.pad(piece_owner.reshape(1, PIECES_DEV), ((0, 0), (0, LANES - PIECES_DEV)))
    box = jnp.pad(piece_box.reshape(1, PIECES_DEV), ((0, 0), (0, LANES - PIECES_DEV)))
    vmem = lambda *shape, dtype=F32: pltpu.VMEM(shape, dtype)
    dma = pltpu.SemaphoreType.DMA
    return pl.pallas_call(
        functools.partial(kernel, members, groups),
        out_shape=(
            jax.ShapeDtypeStruct(fine_state.shape, F32),
            jax.ShapeDtypeStruct((5, 32, BOX_DEV), F32),
        ),
        in_specs=[pl.BlockSpec(memory_space=pl.ANY)] * 4,
        out_specs=[pl.BlockSpec(memory_space=pl.ANY)] * 2,
        scratch_shapes=[
            vmem(5, ROWS, TILES * LANES),
            vmem(5, TILES + 2, 48, LANES),
            vmem(5, 20, ROWS, LANES),
            vmem(5, TILES + 2, ROWS, LANES),
            vmem(5, 40, LANES),
            vmem(5, TILES, LANES),
            vmem(5, 17, ROWS, LANES),
            vmem(5, ROWS, TILES * LANES),
            vmem(5, BOX_DEV, 512),
            vmem(3, 2 * BOX_DEV, 3 * LANES, dtype=BF16),
            vmem(8, LANES, dtype=jnp.int32),
            vmem(LANES, LANES),
            vmem(LANES, LANES),
            vmem(3, LANES, LANES),
            vmem(3, LANES, LANES),
            vmem(LANES, LANES),
            vmem(LANES, LANES),
            vmem(3, LANES, 4 * LANES),
            vmem(3, 4, 32, LANES),
            vmem(2, 5, ROWS, LANES),
            vmem(2, 5, 2, TILES * LANES),
            vmem(5, 32, BOX_DEV),
            dma((4,)),
            dma((2,)),
            dma, dma, dma, dma, dma, dma,
            dma((4,)),
            dma((4,)),
        ],
        compiler_params=pltpu.CompilerParams(
            collective_id=0, has_side_effects=True, vmem_limit_bytes=40 * 1024 * 1024
        ),
    )(fine_state, boxes, owner, box)


def solution(mesh):
    in_specs = (
        P(None, "group", "dev"),
        P(("group", "dev"), None, None),
        P(("group", "dev"), None),
        P(("group", "dev")),
    )
    out_specs = (P(None, "group", "dev"), P(None, None, ("group", "dev")))
    return jax.shard_map(local, mesh=mesh, in_specs=in_specs, out_specs=out_specs, check_vma=False)
```

time: 368 us -> 43.1 us (0.12); the launches traced: 361 us -> 42.9 us
  local copies, waits for them, and re-layouts: 231 us -> 5.65 us
  other arithmetic: 90.8 us -> 0 us
  Pallas kernels: 0 us -> 36.6 us
  starting transfers between devices: 35.5 us -> 0 us
    unnamed x200 -> x6, local copies, waits for them, and re-layouts: 54.4 us -> 4.33 us
    another operation x38 -> x0, local copies, waits for them, and re-layouts: 37.3 us -> none  [the longest x20 16.5 us: state_terms(): jnp.stack(cons_list)]
    pallas_call x0 -> x1, Pallas kernels: none -> 36.6 us  [local(): pl.pallas_call(functools.partial(kernel, members, groups), out_shape=(jax...]
    reshape x7 -> x0, local copies, waits for them, and re-layouts: 27.8 us -> none  [the longest x1 14.6 us: extract(): shaped = box_cells.reshape(box_cells.shape[:-1] + (CB, CB, CB))]
    slice x26 -> x0, local copies, waits for them, and re-layouts: 26.5 us -> none  [the longest x13 11.8 us: part_of(): return lax.slice_in_dim(array, start, stop, axis=dim_index)]
    all_to_all x3 -> x0, starting transfers between devices: 23.7 us -> none  [the longest x1 8.59 us: local(): lax.all_to_all(requests, 'dev', split_axis=0, concat_axis=0, tiled=True)]
    mul x25 -> x0, local copies, waits for them, and re-layouts: 22.4 us -> none  [the longest x4 4.4 us: state_terms(): density * primitive[2]]
    select_n x6 -> x0, local copies, waits for them, and re-layouts: 15.8 us -> none  [the longest x1 11 us: local(): jnp.where(slot_live[..., None, None, None, None], interpolate(coarse_cut,...]
  transfers between devices with their start and end apart: 7 -> 0, of which waited for: 0 -> 0; matrix products, arithmetic and copies ran while one was open for 52% -> 0% of each run, Pallas kernels for 0% -> 0%
where the time goes in v1:
time: 43.1 us; the launch traced here: 42.9 us
  Pallas kernels  36.6 us (85%)
  local copies, waits for them, and re-layouts  5.65 us (13%)
  between operations  0.64 us (1%)
    pallas_call x1, Pallas kernels, local(): pl.pallas_call(functools.partial(kernel, members, groups), out_shape=(jax...  36.6 us
    unnamed x6, local copies, waits for them, and re-layouts  4.33 us

profile of v1, /device:TPU:1, one launch (start us, length us, event | category | flops | bytes accessed | tf_op | source)
XLA Modules:
  0.0 42.9 jit_solution(4059268006646412217)
XLA Ops:
  0.6 0.7 %pad.7.owner_in = s32[1,128]{1,0:T(1,128)S(1)} pad(s32[1,32]{1,0:T(1,128)} %bitcast.4, s32[]{:T(128)} %constant.0.clone.1), padding=0_0x0_96 | pad | bytes 644 | tf_op jit(solution)/shard_map/jit(_pad)/pad | solution.py:497
  1.3 0.7 %pad.8.box_in = s32[1,128]{1,0:T(1,128)S(1)} pad(s32[1,32]{1,0:T(1,128)} %bitcast.5, s32[]{:T(128)} %constant.0.clone.1), padding=0_0x0_96 | pad | bytes 644 | tf_op jit(solution)/shard_map/jit(_pad)/pad | solution.py:498
  2.0 0.0 copy-start
  2.0 1.3 %copy-done = f32[5,32,2048]{2,1,0:T(8,128)S(1)} copy-done((f32[5,32,2048]{2,1,0:T(8,128)S(1)}, f32[5,32,2048]{2,1,0:T(8,128)}, u32[]{:S(2)}) %copy-start) | copy-done | bytes 1310744
  3.3 0.0 copy-start.1
  3.3 1.3 %copy-done.1 = f32[128,5,512]{2,0,1:T(8,128)S(1)} copy-done((f32[128,5,512]{2,0,1:T(8,128)S(1)}, f32[128,5,512]{2,0,1:T(8,128)}, u32[]{:S(2)}) %copy-start.1) | copy-done | bytes 1310744
  4.6 36.6 %shard_map.59 = (f32[5,32,2048]{2,1,0:T(8,128)S(1)}, f32[5,32,128]{2,1,0:T(8,128)S(1)}) custom-call(f32[5,32,2048]{2,1,0:T(8,128)S(1)} %copy-done, f32[5,128,512]{2,1,0:T(8,128)S(1)} %bitcast.3, s32[1,128]{1,0:T(1,128)S(1)} %pad.7.owner_in, s32[1,128]{1,0:T(1,128)S(1)} %pad.8.box_in), custom_call_target="tpu_custom_call" | custom-call | tf_op jit(solution)/shard_map/pallas_call | solution.py:501
  41.2 1.1 %copy.8 = f32[5,32,2048]{2,1,0:T(8,128)} copy(f32[5,32,2048]{2,1,0:T(8,128)S(1)} %get-tuple-element.4) | data formatting | bytes 2621440
  42.3 0.6 %copy.9 = f32[5,32,128]{2,1,0:T(8,128)} copy(f32[5,32,128]{2,1,0:T(8,128)S(1)} %get-tuple-element.5) | data formatting | bytes 163840
Async XLA Ops:
  2.0 1.3 %copy-start = (f32[5,32,2048]{2,1,0:T(8,128)S(1)}, f32[5,32,2048]{2,1,0:T(8,128)}, u32[]{:S(2)}) copy-start(f32[5,32,2048]{2,1,0:T(8,128)} %fine.1) | copy-start | bytes 3932164
  3.3 1.3 %copy-start.1 = (f32[128,5,512]{2,0,1:T(8,128)S(1)}, f32[128,5,512]{2,0,1:T(8,128)}, u32[]{:S(2)}) copy-start(f32[128,5,512]{2,0,1:T(8,128)} %param.5) | copy-start | bytes 3932164

commit v2 on v1

--- a/solution.py
+++ b/solution.py
@@ -104,16 +104,16 @@
     members, groups,
     fine, boxes, owner_in, box_in,
     out, register,
-    q_s, w_s, p_s, fx_s, fy_s, ft_s, fz_s, o_s, cb_s, u_s, ids_s,
-    ask_s, asked_s, give_s, got_s, sum_s, sums_s, ex_s, se_s, xh_s, yh_s, reg_s,
-    load_sem, out_sem, ask_send, ask_recv, give_send, give_recv, sum_send, sum_recv, halo_send, halo_recv,
+    q_s, w_s, p_s, fx_s, fy_s, ft_s, fz_s, cb_s, u_s, owner_s, box_s,
+    ask_s, asked_s, give_s, got_s, sum_s, sums_s, ex_s, se_s, xh_s, yh_s,
+    load_sem, ask_send, ask_recv, give_send, give_recv, sum_send, sum_recv, halo_send, halo_recv,
 ):
     me = lax.axis_index("dev")
     group = lax.axis_index("group")
 
     load_ids = [
-        pltpu.make_async_copy(owner_in, ids_s.at[0:1], load_sem.at[0]),
-        pltpu.make_async_copy(box_in, ids_s.at[1:2], load_sem.at[1]),
+        pltpu.make_async_copy(owner_in, owner_s, load_sem.at[0]),
+        pltpu.make_async_copy(box_in, box_s, load_sem.at[1]),
     ]
     load_boxes = pltpu.make_async_copy(boxes, cb_s, load_sem.at[2])
     load_fine = pltpu.make_async_copy(fine, q_s, load_sem.at[3])
@@ -144,8 +144,9 @@
     for copy in load_ids:
         copy.wait()
     live = lane1 < PIECES_DEV
-    owner = jnp.where(live, ids_s[0:1, :], -1)
-    box = ids_s[1:2, :]
+    fill = jnp.full((1, LANES - PIECES_DEV), -1, jnp.int32)
+    owner = jnp.concatenate([owner_s[...], fill], axis=1)
+    box = jnp.concatenate([box_s[...], fill], axis=1)
     row32, lane32 = iota((PIECES_DEV, LANES), 0), iota((PIECES_DEV, LANES), 1)
     owner_f = owner.astype(F32)
     owner_all = jnp.broadcast_to(owner_f, (PIECES_DEV, LANES))
@@ -270,7 +271,7 @@
                     u_s[i, where, pair * LANES : (pair + 1) * LANES] = x
         return c
 
-    lax.fori_loop(0, BOX_DEV // 16, table, 0)
+    lax.fori_loop(0, BOX_DEV // 16, table, 0, unroll=4)
 
     load_fine.wait()
 
@@ -311,7 +312,7 @@
             p_s[f, 2 + z, pl.ds(pl.multiple_of(rb * 8, 8), 8), :] = tiles[z]
         return c
 
-    lax.fori_loop(0, 20, pack, 0)
+    lax.fori_loop(0, 20, pack, 0, unroll=4)
 
     def z_face(k, half):
         rows = slice(16 * half, 16 * half + 16)
@@ -391,7 +392,7 @@
             low, high = fx_s[f, t + 1], fx_s[f, t + 2]
             dx = pltpu.roll(jnp.where(lane_r < 16, high, low), LANES - 16, 1) - low
             dy = fy_s[f, 1 : 1 + ROWS, :] - fy_s[f, 0:ROWS, :]
-            o_s[f, :, lanes] = q_s[f, :, lanes] - DT_DX * (dx + dy)
+            out[f, :, lanes] = q_s[f, :, lanes] - DT_DX * (dx + dy)
         return c
 
     lax.fori_loop(0, TILES, y_faces, 0)
@@ -471,41 +472,35 @@
         tiles = swap_tiles([z[k + 1] - z[k] for k in range(16)])
         for t in range(TILES):
             lanes = slice(t * LANES, (t + 1) * LANES)
-            o_s[f, rows, lanes] = o_s[f, rows, lanes] - DT_DX * tiles[t]
-        return c
-
-    lax.fori_loop(0, 20, finish, 0)
-    store = pltpu.make_async_copy(o_s, out, out_sem.at[0])
-    store.start()
+            out[f, rows, lanes] = out[f, rows, lanes] - DT_DX * tiles[t]
+        return c
+
+    lax.fori_loop(0, 20, finish, 0, unroll=4)
 
     all_of(sums_s, sum_send, sum_recv, rest).wait()
     total = sum(dot(x, chosen, 0, 0) for x in parts(sums_s[...]))
     for f in range(5):
         for s in range(2):
-            reg_s[f, 16 * s : 16 * s + 16, :] = total[
+            register[f, 16 * s : 16 * s + 16, :] = total[
                 16 * f : 16 * f + 16, s * LANES : (s + 1) * LANES
             ]
-    store_register = pltpu.make_async_copy(reg_s, register, out_sem.at[1])
-    store_register.start()
-    store.wait()
-    store_register.wait()
 
 
 def local(fine_state, coarse_boxes, piece_owner, piece_box):
     members, groups = lax.axis_size("dev"), lax.axis_size("group")
     boxes = coarse_boxes.transpose(1, 0, 2)
-    owner = jnp.pad(piece_owner.reshape(1, PIECES_DEV), ((0, 0), (0, LANES - PIECES_DEV)))
-    box = jnp.pad(piece_box.reshape(1, PIECES_DEV), ((0, 0), (0, LANES - PIECES_DEV)))
+    owner = piece_owner.reshape(1, PIECES_DEV)
+    box = piece_box.reshape(1, PIECES_DEV)
     vmem = lambda *shape, dtype=F32: pltpu.VMEM(shape, dtype)
     dma = pltpu.SemaphoreType.DMA
     return pl.pallas_call(
         functools.partial(kernel, members, groups),
         out_shape=(
-            jax.ShapeDtypeStruct(fine_state.shape, F32),
-            jax.ShapeDtypeStruct((5, 32, BOX_DEV), F32),
+            vmem(*fine_state.shape),
+            vmem(5, 32, BOX_DEV),
         ),
-        in_specs=[pl.BlockSpec(memory_space=pl.ANY)] * 4,
-        out_specs=[pl.BlockSpec(memory_space=pl.ANY)] * 2,
+        in_specs=[pl.BlockSpec(memory_space=pltpu.HBM)] * 4,
+        out_specs=[pl.BlockSpec(memory_space=pltpu.VMEM)] * 2,
         scratch_shapes=[
             vmem(5, ROWS, TILES * LANES),
             vmem(5, TILES + 2, 48, LANES),
@@ -514,10 +509,10 @@
             vmem(5, 40, LANES),
             vmem(5, TILES, LANES),
             vmem(5, 17, ROWS, LANES),
-            vmem(5, ROWS, TILES * LANES),
             vmem(5, BOX_DEV, 512),
             vmem(3, 2 * BOX_DEV, 3 * LANES, dtype=BF16),
-            vmem(8, LANES, dtype=jnp.int32),
+            vmem(1, PIECES_DEV, dtype=jnp.int32),
+            vmem(1, PIECES_DEV, dtype=jnp.int32),
             vmem(LANES, LANES),
             vmem(LANES, LANES),
             vmem(3, LANES, LANES),
@@ -528,9 +523,7 @@
             vmem(3, 4, 32, LANES),
             vmem(2, 5, ROWS, LANES),
             vmem(2, 5, 2, TILES * LANES),
-            vmem(5, 32, BOX_DEV),
             dma((4,)),
-            dma((2,)),
             dma, dma, dma, dma, dma, dma,
             dma((4,)),
             dma((4,)),
@@ -538,7 +531,7 @@
         compiler_params=pltpu.CompilerParams(
             collective_id=0, has_side_effects=True, vmem_limit_bytes=40 * 1024 * 1024
         ),
-    )(fine_state, boxes, owner, box)
+    )(*[pltpu.with_memory_space_constraint(x, pltpu.HBM) for x in (fine_state, boxes, owner, box)])
 
 
 def solution(mesh):

time: 43.1 us -> 32.3 us (0.75)
  Pallas kernels: 36.6 us -> 29.8 us
  local copies, waits for them, and re-layouts: 5.65 us -> 1.69 us
    pallas_call x1, Pallas kernels: 36.6 us -> 29.8 us  [local(): pl.pallas_call(functools.partial(kernel, members, groups), out_shape=(vme...]
    unnamed x6 -> x2, local copies, waits for them, and re-layouts: 4.33 us -> 1.69 us
    pad x2 -> x0, local copies, waits for them, and re-layouts: 1.32 us -> none  [the longest x1 0.66 us: local(): jnp.pad(piece_owner.reshape(1, PIECES_DEV), ((0, 0), (0, LANES - PIECES_D...]
where the time goes in v2:
time: 32.3 us; the launch traced here: 32.2 us
  Pallas kernels  29.8 us (92%)
  local copies, waits for them, and re-layouts  1.69 us (5%)
  between operations  0.64 us (2%)
    pallas_call x1, Pallas kernels, local(): pl.pallas_call(functools.partial(kernel, members, groups), out_shape=(vme...  29.8 us
    unnamed x2, local copies, waits for them, and re-layouts  1.69 us

profile of v2, /device:TPU:1, one launch (start us, length us, event | category | flops | bytes accessed | tf_op | source)
XLA Modules:
  0.0 32.2 jit_solution(2282320740663999534)
XLA Ops:
  0.6 29.8 %shard_map.59 = (f32[5,32,2048]{2,1,0:T(8,128)S(1)}, f32[5,32,128]{2,1,0:T(8,128)S(1)}) custom-call(f32[5,32,2048]{2,1,0:T(8,128)} %fine.1, f32[5,128,512]{2,1,0:T(8,128)} %bitcast.3, s32[1,32]{1,0:T(1,128)} %bitcast.4, s32[1,32]{1,0:T(1,128)} %bitcast.5), custom_call_target="tpu_custom_call" | custom-call | tf_op jit(solution)/shard_map/pallas_call | solution.py:496
  30.5 1.1 %copy.8 = f32[5,32,2048]{2,1,0:T(8,128)} copy(f32[5,32,2048]{2,1,0:T(8,128)S(1)} %get-tuple-element.2) | data formatting | bytes 2621440
  31.5 0.6 %copy.9 = f32[5,32,128]{2,1,0:T(8,128)} copy(f32[5,32,128]{2,1,0:T(8,128)S(1)} %get-tuple-element.3) | data formatting | bytes 163840

commit v3 on v2

--- a/solution.py
+++ b/solution.py
@@ -284,6 +284,16 @@
 
     lax.fori_loop(0, TILES, to_primitive, 0)
 
+    def pack(n, c):
+        f, rb = n // 4, n % 4
+        rows = pl.ds(pl.multiple_of(8 + rb * 8, 8), 8)
+        tiles = swap_tiles([w_s[f, 1 + t, rows, :] for t in range(TILES)])
+        for z in range(16):
+            p_s[f, 2 + z, pl.ds(pl.multiple_of(rb * 8, 8), 8), :] = tiles[z]
+        return c
+
+    lax.fori_loop(0, 20, pack, 0, unroll=4)
+
     all_of(asked_s, ask_send, ask_recv, rest).wait()
     asked = asked_s[...]
     lane_f = lane128.astype(F32)
@@ -303,16 +313,6 @@
         give_s[pair] = give[:, pair * LANES : (pair + 1) * LANES]
     exchange(give_s, got_s, give_send, give_recv, -1, one3)
     got_s[:, 0:MOST, :] = give_s[:, 0:MOST, :]
-
-    def pack(n, c):
-        f, rb = n // 4, n % 4
-        rows = pl.ds(pl.multiple_of(8 + rb * 8, 8), 8)
-        tiles = swap_tiles([w_s[f, 1 + t, rows, :] for t in range(TILES)])
-        for z in range(16):
-            p_s[f, 2 + z, pl.ds(pl.multiple_of(rb * 8, 8), 8), :] = tiles[z]
-        return c
-
-    lax.fori_loop(0, 20, pack, 0, unroll=4)
 
     def z_face(k, half):
         rows = slice(16 * half, 16 * half + 16)
@@ -373,29 +373,6 @@
         return c
 
     lax.fori_loop(1, TILES + 2, x_faces, 0)
-
-    top = face(*[[w_s[f, 1 : 1 + TILES, 38 + i, :] for f in range(5)] for i in range(4)], 1)
-    for f in range(5):
-        ft_s[f] = top[f]
-
-    def y_faces(t, c):
-        lanes = pl.ds(pl.multiple_of(t * LANES, LANES), LANES)
-        for half in range(2):
-            first = 6 + 16 * half
-            w = [[w_s[f, t + 1, first + i : first + i + 16, :] for f in range(5)] for i in range(4)]
-            flux = face(*w, 1)
-            for f in range(5):
-                fy_s[f, 16 * half : 16 * half + 16, :] = flux[f]
-        for f in range(5):
-            fy_s[f, ROWS : ROWS + 1, :] = ft_s[f, pl.ds(t, 1), :]
-        for f in range(5):
-            low, high = fx_s[f, t + 1], fx_s[f, t + 2]
-            dx = pltpu.roll(jnp.where(lane_r < 16, high, low), LANES - 16, 1) - low
-            dy = fy_s[f, 1 : 1 + ROWS, :] - fy_s[f, 0:ROWS, :]
-            out[f, :, lanes] = q_s[f, :, lanes] - DT_DX * (dx + dy)
-        return c
-
-    lax.fori_loop(0, TILES, y_faces, 0)
 
     all_of(got_s, give_send, give_recv, rest3).wait()
     for pair in range(3):
@@ -464,6 +441,29 @@
     for k in (1, 15):
         z_face(k, 0)
         z_face(k, 1)
+
+    top = face(*[[w_s[f, 1 : 1 + TILES, 38 + i, :] for f in range(5)] for i in range(4)], 1)
+    for f in range(5):
+        ft_s[f] = top[f]
+
+    def y_faces(t, c):
+        lanes = pl.ds(pl.multiple_of(t * LANES, LANES), LANES)
+        for half in range(2):
+            first = 6 + 16 * half
+            w = [[w_s[f, t + 1, first + i : first + i + 16, :] for f in range(5)] for i in range(4)]
+            flux = face(*w, 1)
+            for f in range(5):
+                fy_s[f, 16 * half : 16 * half + 16, :] = flux[f]
+        for f in range(5):
+            fy_s[f, ROWS : ROWS + 1, :] = ft_s[f, pl.ds(t, 1), :]
+        for f in range(5):
+            low, high = fx_s[f, t + 1], fx_s[f, t + 2]
+            dx = pltpu.roll(jnp.where(lane_r < 16, high, low), LANES - 16, 1) - low
+            dy = fy_s[f, 1 : 1 + ROWS, :] - fy_s[f, 0:ROWS, :]
+            out[f, :, lanes] = q_s[f, :, lanes] - DT_DX * (dx + dy)
+        return c
+
+    lax.fori_loop(0, TILES, y_faces, 0)
 
     def finish(n, c):
         f, rb = n // 4, n % 4

time: 32.3 us -> 30.9 us (0.957)
  Pallas kernels: 29.8 us -> 28.4 us
    pallas_call x1, Pallas kernels: 29.8 us -> 28.4 us  [local(): pl.pallas_call(functools.partial(kernel, members, groups), out_shape=(vme...]
where the time goes in v3:
time: 30.9 us; the launch traced here: 30.8 us
  Pallas kernels  28.4 us (92%)
  local copies, waits for them, and re-layouts  1.69 us (5%)
  between operations  0.64 us (2%)
    pallas_call x1, Pallas kernels, local(): pl.pallas_call(functools.partial(kernel, members, groups), out_shape=(vme...  28.4 us
    unnamed x2, local copies, waits for them, and re-layouts  1.69 us

profile of v3, /device:TPU:1, one launch (start us, length us, event | category | flops | bytes accessed | tf_op | source)
XLA Modules:
  0.0 30.8 jit_solution(7860200418546449188)
XLA Ops:
  0.6 28.4 %shard_map.59 = (f32[5,32,2048]{2,1,0:T(8,128)S(1)}, f32[5,32,128]{2,1,0:T(8,128)S(1)}) custom-call(f32[5,32,2048]{2,1,0:T(8,128)} %fine.1, f32[5,128,512]{2,1,0:T(8,128)} %bitcast.3, s32[1,32]{1,0:T(1,128)} %bitcast.4, s32[1,32]{1,0:T(1,128)} %bitcast.5), custom_call_target="tpu_custom_call" | custom-call | tf_op jit(solution)/shard_map/pallas_call | solution.py:496
  29.1 1.1 %copy.8 = f32[5,32,2048]{2,1,0:T(8,128)} copy(f32[5,32,2048]{2,1,0:T(8,128)S(1)} %get-tuple-element.2) | data formatting | bytes 2621440
  30.1 0.6 %copy.9 = f32[5,32,128]{2,1,0:T(8,128)} copy(f32[5,32,128]{2,1,0:T(8,128)S(1)} %get-tuple-element.3) | data formatting | bytes 163840

commit v4 on v3

--- a/solution.py
+++ b/solution.py
@@ -163,75 +163,6 @@
     )
     ask_s[...] = jnp.broadcast_to(asked_value, (LANES, LANES))
 
-    pl.semaphore_wait(barrier, members + 1)
-
-    def exchange(buffer, landed, send, recv, sign, part):
-        def copy(k):
-            return pltpu.make_async_remote_copy(
-                src_ref=part(buffer, k),
-                dst_ref=part(landed, k),
-                send_sem=send,
-                recv_sem=recv,
-                device_id=(group, lax.rem(me + sign * k + members, members)),
-                device_id_type=MESH,
-            )
-
-        def start(k, c):
-            copy(k).start()
-            return c
-
-        lax.fori_loop(1, members, start, 0)
-
-    def all_of(landed, send, recv, part):
-        whole = part(landed)
-        return pltpu.make_async_remote_copy(
-            src_ref=whole, dst_ref=whole, send_sem=send, recv_sem=recv,
-            device_id=(group, lax.rem(me + 1, members)), device_id_type=MESH,
-        )
-
-    one = lambda ref, k: ref.at[pl.ds(k * MOST, MOST)]
-    one3 = lambda ref, k: ref.at[:, pl.ds(k * MOST, MOST)]
-    rest = lambda ref: ref.at[pl.ds(MOST, (members - 1) * MOST)]
-    rest3 = lambda ref: ref.at[:, pl.ds(MOST, (members - 1) * MOST)]
-
-    exchange(ask_s, asked_s, ask_send, ask_recv, 1, one)
-    asked_s[0:MOST, :] = ask_s[0:MOST, :]
-
-    right, left = lax.rem(me + 1, members), lax.rem(me + members - 1, members)
-    last = fine.shape[2] - LANES
-    halos = [
-        (fine.at[:, :, pl.ds(last, LANES)], xh_s.at[0], (group, right)),
-        (fine.at[:, :, pl.ds(0, LANES)], xh_s.at[1], (group, left)),
-        (fine.at[:, pl.ds(ROWS - 2, 2)], yh_s.at[0], (north, me)),
-        (fine.at[:, pl.ds(0, 2)], yh_s.at[1], (south, me)),
-    ]
-    halo_copies = [
-        pltpu.make_async_remote_copy(
-            src_ref=src, dst_ref=dst, send_sem=halo_send.at[i], recv_sem=halo_recv.at[i],
-            device_id=target, device_id_type=MESH,
-        )
-        for i, (src, dst, target) in enumerate(halos)
-    ]
-    for copy in halo_copies:
-        copy.start()
-
-    spots = []
-    for ky in range(2):
-        v = slot if ky == 0 else pltpu.roll(slot, LANES - 16, 1)
-        v = jnp.where(lane1 < 16, v, 0)
-        for step in (16, 32, 64):
-            v = v + pltpu.roll(v, step, 1)
-        odd = (lane1 & 1) != 0
-        spots.append(jnp.where(odd, pltpu.roll(v, 1, 1), v))
-        spots.append(jnp.where(odd, v, pltpu.roll(v, LANES - 1, 1)))
-    spot = jnp.concatenate(
-        [
-            jnp.where(row128 == jnp.broadcast_to(s, (LANES, LANES)), 1.0, 0.0).astype(BF16)
-            for s in spots
-        ],
-        axis=1,
-    )
-
     load_boxes.wait()
 
     def table(n, c):
@@ -271,7 +202,78 @@
                     u_s[i, where, pair * LANES : (pair + 1) * LANES] = x
         return c
 
-    lax.fori_loop(0, BOX_DEV // 16, table, 0, unroll=4)
+    lax.fori_loop(0, BOX_DEV // 32, table, 0, unroll=4)
+
+    pl.semaphore_wait(barrier, members + 1)
+
+    def exchange(buffer, landed, send, recv, sign, part):
+        def copy(k):
+            return pltpu.make_async_remote_copy(
+                src_ref=part(buffer, k),
+                dst_ref=part(landed, k),
+                send_sem=send,
+                recv_sem=recv,
+                device_id=(group, lax.rem(me + sign * k + members, members)),
+                device_id_type=MESH,
+            )
+
+        def start(k, c):
+            copy(k).start()
+            return c
+
+        lax.fori_loop(1, members, start, 0)
+
+    def all_of(landed, send, recv, part):
+        whole = part(landed)
+        return pltpu.make_async_remote_copy(
+            src_ref=whole, dst_ref=whole, send_sem=send, recv_sem=recv,
+            device_id=(group, lax.rem(me + 1, members)), device_id_type=MESH,
+        )
+
+    one = lambda ref, k: ref.at[pl.ds(k * MOST, MOST)]
+    one3 = lambda ref, k: ref.at[:, pl.ds(k * MOST, MOST)]
+    rest = lambda ref: ref.at[pl.ds(MOST, (members - 1) * MOST)]
+    rest3 = lambda ref: ref.at[:, pl.ds(MOST, (members - 1) * MOST)]
+
+    exchange(ask_s, asked_s, ask_send, ask_recv, 1, one)
+    asked_s[0:MOST, :] = ask_s[0:MOST, :]
+
+    right, left = lax.rem(me + 1, members), lax.rem(me + members - 1, members)
+    last = fine.shape[2] - LANES
+    halos = [
+        (fine.at[:, :, pl.ds(last, LANES)], xh_s.at[0], (group, right)),
+        (fine.at[:, :, pl.ds(0, LANES)], xh_s.at[1], (group, left)),
+        (fine.at[:, pl.ds(ROWS - 2, 2)], yh_s.at[0], (north, me)),
+        (fine.at[:, pl.ds(0, 2)], yh_s.at[1], (south, me)),
+    ]
+    halo_copies = [
+        pltpu.make_async_remote_copy(
+            src_ref=src, dst_ref=dst, send_sem=halo_send.at[i], recv_sem=halo_recv.at[i],
+            device_id=target, device_id_type=MESH,
+        )
+        for i, (src, dst, target) in enumerate(halos)
+    ]
+    for copy in halo_copies:
+        copy.start()
+
+    spots = []
+    for ky in range(2):
+        v = slot if ky == 0 else pltpu.roll(slot, LANES - 16, 1)
+        v = jnp.where(lane1 < 16, v, 0)
+        for step in (16, 32, 64):
+            v = v + pltpu.roll(v, step, 1)
+        odd = (lane1 & 1) != 0
+        spots.append(jnp.where(odd, pltpu.roll(v, 1, 1), v))
+        spots.append(jnp.where(odd, v, pltpu.roll(v, LANES - 1, 1)))
+    spot = jnp.concatenate(
+        [
+            jnp.where(row128 == jnp.broadcast_to(s, (LANES, LANES)), 1.0, 0.0).astype(BF16)
+            for s in spots
+        ],
+        axis=1,
+    )
+
+    lax.fori_loop(BOX_DEV // 32, BOX_DEV // 16, table, 0, unroll=4)
 
     load_fine.wait()
 

time: 30.9 us -> 28.8 us (0.932)
  Pallas kernels: 28.4 us -> 26.3 us
    pallas_call x1, Pallas kernels: 28.4 us -> 26.3 us  [local(): pl.pallas_call(functools.partial(kernel, members, groups), out_shape=(vme...]
where the time goes in v4:
time: 28.8 us; the launch traced here: 28.7 us
  Pallas kernels  26.3 us (91%)
  local copies, waits for them, and re-layouts  1.69 us (6%)
  between operations  0.64 us (2%)
    pallas_call x1, Pallas kernels, local(): pl.pallas_call(functools.partial(kernel, members, groups), out_shape=(vme...  26.3 us
    unnamed x2, local copies, waits for them, and re-layouts  1.69 us

profile of v4, /device:TPU:1, one launch (start us, length us, event | category | flops | bytes accessed | tf_op | source)
XLA Modules:
  0.0 28.7 jit_solution(2638432531302496462)
XLA Ops:
  0.6 26.3 %shard_map.59 = (f32[5,32,2048]{2,1,0:T(8,128)S(1)}, f32[5,32,128]{2,1,0:T(8,128)S(1)}) custom-call(f32[5,32,2048]{2,1,0:T(8,128)} %fine.1, f32[5,128,512]{2,1,0:T(8,128)} %bitcast.3, s32[1,32]{1,0:T(1,128)} %bitcast.4, s32[1,32]{1,0:T(1,128)} %bitcast.5), custom_call_target="tpu_custom_call" | custom-call | tf_op jit(solution)/shard_map/pallas_call | solution.py:498
  27.0 1.1 %copy.8 = f32[5,32,2048]{2,1,0:T(8,128)} copy(f32[5,32,2048]{2,1,0:T(8,128)S(1)} %get-tuple-element.2) | data formatting | bytes 2621440
  28.0 0.6 %copy.9 = f32[5,32,128]{2,1,0:T(8,128)} copy(f32[5,32,128]{2,1,0:T(8,128)S(1)} %get-tuple-element.3) | data formatting | bytes 163840

commit v5 on v4

--- a/solution.py
+++ b/solution.py
@@ -204,6 +204,17 @@
 
     lax.fori_loop(0, BOX_DEV // 32, table, 0, unroll=4)
 
+    load_fine.wait()
+
+    def to_primitive(t, c):
+        lanes = pl.ds(pl.multiple_of(t * LANES, LANES), LANES)
+        w = primitives([q_s[f, :, lanes] for f in range(5)])
+        for f in range(5):
+            w_s[f, t + 1, 8 : 8 + ROWS, :] = w[f]
+        return c
+
+    lax.fori_loop(0, TILES, to_primitive, 0)
+
     pl.semaphore_wait(barrier, members + 1)
 
     def exchange(buffer, landed, send, recv, sign, part):
@@ -275,16 +286,6 @@
 
     lax.fori_loop(BOX_DEV // 32, BOX_DEV // 16, table, 0, unroll=4)
 
-    load_fine.wait()
-
-    def to_primitive(t, c):
-        lanes = pl.ds(pl.multiple_of(t * LANES, LANES), LANES)
-        w = primitives([q_s[f, :, lanes] for f in range(5)])
-        for f in range(5):
-            w_s[f, t + 1, 8 : 8 + ROWS, :] = w[f]
-        return c
-
-    lax.fori_loop(0, TILES, to_primitive, 0)
 
     def pack(n, c):
         f, rb = n // 4, n % 4
@@ -296,7 +297,8 @@
 
     lax.fori_loop(0, 20, pack, 0, unroll=4)
 
-    all_of(asked_s, ask_send, ask_recv, rest).wait()
+    asks = all_of(asked_s, ask_send, ask_recv, rest)
+    asks.wait_recv()
     asked = asked_s[...]
     lane_f = lane128.astype(F32)
     chosen = jnp.concatenate(
@@ -331,7 +333,7 @@
     lax.fori_loop(2, 15, z_inner, 0)
 
     for copy in halo_copies:
-        copy.wait()
+        copy.wait_recv()
     lane_r = iota((ROWS, LANES), 1)
     x_low = primitives([xh_s[0, f] for f in range(5)])
     x_high = primitives([xh_s[1, f] for f in range(5)])
@@ -376,7 +378,8 @@
 
     lax.fori_loop(1, TILES + 2, x_faces, 0)
 
-    all_of(got_s, give_send, give_recv, rest3).wait()
+    gifts = all_of(got_s, give_send, give_recv, rest3)
+    gifts.wait_recv()
     for pair in range(3):
         got = parts(got_s[pair])
         ex_s[pair] = sum(dot(x, spot, 0, 0) for x in got)
@@ -465,7 +468,7 @@
             out[f, :, lanes] = q_s[f, :, lanes] - DT_DX * (dx + dy)
         return c
 
-    lax.fori_loop(0, TILES, y_faces, 0)
+    lax.fori_loop(0, TILES, y_faces, 0, unroll=2)
 
     def finish(n, c):
         f, rb = n // 4, n % 4
@@ -479,13 +482,16 @@
 
     lax.fori_loop(0, 20, finish, 0, unroll=4)
 
-    all_of(sums_s, sum_send, sum_recv, rest).wait()
+    totals = all_of(sums_s, sum_send, sum_recv, rest)
+    totals.wait_recv()
     total = sum(dot(x, chosen, 0, 0) for x in parts(sums_s[...]))
     for f in range(5):
         for s in range(2):
             register[f, 16 * s : 16 * s + 16, :] = total[
                 16 * f : 16 * f + 16, s * LANES : (s + 1) * LANES
             ]
+    for copy in (asks, gifts, totals, *halo_copies):
+        copy.wait_send()
 
 
 def local(fine_state, coarse_boxes, piece_owner, piece_box):

time: 28.8 us -> 28.6 us (level)
  no operation moved by 1% of the time
where the time goes in v5:
time: 28.6 us; the launch traced here: 28.5 us
  Pallas kernels  26.1 us (91%)
  local copies, waits for them, and re-layouts  1.69 us (6%)
  between operations  0.64 us (2%)
    pallas_call x1, Pallas kernels, local(): pl.pallas_call(functools.partial(kernel, members, groups), out_shape=(vme...  26.1 us
    unnamed x2, local copies, waits for them, and re-layouts  1.69 us

profile of v5, /device:TPU:1, one launch (start us, length us, event | category | flops | bytes accessed | tf_op | source)
XLA Modules:
  0.0 28.5 jit_solution(9882853023464903637)
XLA Ops:
  0.6 26.1 %shard_map.59 = (f32[5,32,2048]{2,1,0:T(8,128)S(1)}, f32[5,32,128]{2,1,0:T(8,128)S(1)}) custom-call(f32[5,32,2048]{2,1,0:T(8,128)} %fine.1, f32[5,128,512]{2,1,0:T(8,128)} %bitcast.3, s32[1,32]{1,0:T(1,128)} %bitcast.4, s32[1,32]{1,0:T(1,128)} %bitcast.5), custom_call_target="tpu_custom_call" | custom-call | tf_op jit(solution)/shard_map/pallas_call | solution.py:504
  26.8 1.1 %copy.8 = f32[5,32,2048]{2,1,0:T(8,128)} copy(f32[5,32,2048]{2,1,0:T(8,128)S(1)} %get-tuple-element.2) | data formatting | bytes 2621440
  27.8 0.6 %copy.9 = f32[5,32,128]{2,1,0:T(8,128)} copy(f32[5,32,128]{2,1,0:T(8,128)S(1)} %get-tuple-element.3) | data formatting | bytes 163840
